TPU v7x, 512 devices: a whole 4x8x8 slice. The times are simulated.
512 devices in a mesh: ops: 64 (over y_hi, z, core), blk: 8 (over x, y_lo).
Axes of the slice: x: 4, y: 8 (y_hi: 4, y_lo: 2; y = y_hi * 2 + y_lo), z: 8, core: 2. Of those that a mesh axis runs over, the one named last changes fastest.
Arguments:
- wave: float32 [384, 16, 384], P('ops', 'blk'), may hold values from -6 to 6
- left_op: float32 [128, 16, 384, 384], P('ops', 'blk'), may hold values from -1 to 13
- right_op: float32 [128, 16, 384, 384], P('ops', 'blk'), may hold values from -1 to 1
- left_dims: int32 [16], P('blk'), may hold values from 1 to 384, 2048 in all
- right_dims: int32 [16], P('blk'), may hold values from 1 to 384, 2048 in all
Outputs:
- sigma: float32 [384, 16, 384], P('ops', 'blk')
- residual: float32 [384, 16, 384], P('ops', 'blk')
Inputs may be any that keep to these rules, and one draw needn't show every extreme that they name: `left_dims`: each sums to 2048; the largest is exactly 384. `right_dims`: each sums to 2048; the largest is exactly 384.
All inputs are finite; a program needn't handle non-finite values. No bound on the sum of `left_dims` or of `right_dims` on one device may be relied on, other than what follows from the above.
Results may differ from a plain program's by a relative error of at most 0.00029.
Values sent between devices are 32-bit elements; how exact they have to be, the bound alone decides.
A program may use at most 64 MiB of HBM per device.

v0:
```python
import jax
import jax.numpy as jnp
from jax import lax
from jax.sharding import PartitionSpec as P

CAP = 384


def sector_mask(left_dims, right_dims, offset, rows):
    row_ids = offset + jnp.arange(rows, dtype=jnp.int32)
    col_ids = jnp.arange(CAP, dtype=jnp.int32)
    inside = (row_ids[:, None, None] < left_dims[None, :, None]) & (
        col_ids[None, None, :] < right_dims[None, :, None]
    )
    return inside.astype(jnp.float32)


def late_sums(psi_local, sigma_local):
    return lax.psum(
        (jnp.sum(psi_local * psi_local), jnp.sum(psi_local * sigma_local)), ("blk", "ops")
    )


def local(wave, left_op, right_op, left_dims, right_dims):
    own_rows = wave.shape[0]
    offset = lax.axis_index("ops") * own_rows
    mask_local = sector_mask(left_dims, right_dims, offset, own_rows)
    psi_local = wave * mask_local
    highest = lax.Precision.HIGHEST
    gathered = lax.all_gather(wave, "ops", axis=0, tiled=True)
    psi_whole = gathered * sector_mask(left_dims, right_dims, jnp.int32(0), gathered.shape[0])
    inner = jnp.einsum("tsik,ksj->tisj", left_op, psi_whole, precision=highest)
    partial_sigma = jnp.einsum("tisk,tsjk->isj", inner, right_op, precision=highest)
    sigma_local = (
        lax.psum_scatter(partial_sigma, "ops", scatter_dimension=0, tiled=True) * mask_local
    )
    norm, correlation = late_sums(psi_local, sigma_local)
    theta = correlation / norm
    residual = sigma_local - theta * psi_local
    return (sigma_local, residual)


def solution(mesh):
    in_specs = (
        P("ops", "blk", None),
        P("ops", "blk", None, None),
        P("ops", "blk", None, None),
        P("blk"),
        P("blk"),
    )
    out_specs = (P("ops", "blk", None), P("ops", "blk", None))
    return jax.shard_map(local, mesh=mesh, in_specs=in_specs, out_specs=out_specs, check_vma=False)
```

profile of v0, /device:TPU:1, one launch (start us, length us, event | category | flops | bytes accessed | tf_op | source)
XLA Modules:
  0.0 756.0 jit_solution(473572362820747170)
XLA Ops:
  7.2 0.0 copy-start
  7.2 0.0 all-gather.2.cloned.1.call-start
  7.2 0.7 all-gather.2.cloned.1.call-update
  7.9 0.0 all-reduce.4.cloned.1.call-start
  8.0 0.7 iota_compare_fusion.1
  8.7 0.7 iota_compare_fusion
  9.4 91.0 %all-gather.2.cloned.1.call-done = f32[384,2,384]{2,1,0:T(2,128)} async-done(((f32[6,2,384]{2,1,0:T(2,128)}), f32[384,2,384]{2,1,0:T(2,128)}) %all-gather.2.cloned.1.call-update) | async-done | bytes 1179664 | tf_op jit(solution)/shard_map/all_gather | solution.py:30
  100.4 1.9 fusion.10
  102.3 0.0 copy-done
  102.3 0.0 copy-start.1
  102.3 4.7 fusion.2
  107.0 0.0 copy-done.1
  107.0 4.0 fusion.5
  111.0 0.0 copy-start.4
  111.0 0.0 copy-start.2
  111.0 2.0 copy.12
  113.0 0.0 all-reduce.4.cloned.1.call-update
  113.0 1.3 dynamic-slice
  115.0 0.0 copy-done.4
  115.0 0.1 broadcast_compare_fusion
  115.0 531.2 %all-reduce.4.cloned.1.call-done = f32[384,2,384]{2,1,0:T(2,128)} async-done(((f32[384,2,384]{2,1,0:T(2,128)}), f32[384,2,384]{2,1,0:T(2,128)}) %all-reduce.4.cloned.1.call-update) | async-done | bytes 1179664
  646.2 0.0 copy-done.2
  646.2 1.5 multiply_reduce_fusion
  647.7 0.0 copy-start.3
  647.7 99.4 %all-reduce.1 = (f32[]{:T(128)}, f32[]{:T(128)}) all-reduce(f32[]{:T(128)} %get-tuple-element.5, f32[]{:T(128)} %get-tuple-element.4), channel_id=1, replica_groups=mesh['ops'=64,'blk'=8] {'blk','ops'}, use_global_device_ids=true, to_apply=%region_2.0 | all-reduce | flops 2 | bytes 16 | tf_op jit(solution)/shard_map/psum | solution.py:19
  748.4 0.7 multiply_subtract_fusion
  749.1 0.0 copy-done.3
  (1 shorter events, 0.0 us)
Async XLA Ops:
  7.2 95.1 %copy-start = (f32[2,2,384,384]{3,2,1,0:T(8,128)S(1)}, f32[2,2,384,384]{3,2,1,0:T(8,128)}, u32[]{:S(2)}) copy-start(f32[2,2,384,384]{3,2,1,0:T(8,128)} %param.6) | copy-start | bytes 7077892
  7.2 93.2 %all-gather.2.cloned.1.call-start = ((), (), s32[]{:S(2)}) async-start(), calls=%async_computation | async-start | bytes 1198080 | tf_op jit(solution)/shard_map/all_gather | solution.py:30
  7.9 638.3 %all-reduce.4.cloned.1.call-start = ((), (), s32[]{:S(2)}) async-start(), calls=%async_computation.1 | async-start | bytes 2359296
  102.3 4.7 copy-start.1
  111.0 4.0 copy-start.4
  111.0 535.2 %copy-start.2 = (f32[6,2,384]{2,1,0:T(2,128)S(1)}, f32[6,2,384]{2,1,0:T(2,128)}, u32[]{:S(2)}) copy-start(f32[6,2,384]{2,1,0:T(2,128)} %param.5) | copy-start | bytes 55300
  647.7 101.4 %copy-start.3 = (f32[6,2,384]{2,1,0:T(2,128)}, f32[6,2,384]{2,1,0:T(2,128)S(1)}, u32[]{:S(2)}) copy-start(f32[6,2,384]{2,1,0:T(2,128)S(1)} %get-tuple-element.8) | copy-start | bytes 55300
Sparse Core Ops, SparseCore 0:
  11.3 89.0 all-gather.1
  113.1 533.0 all-reduce.3
where the time goes:
time: 756 us
  waiting for transfers between devices  623 us (82%)
  blocking collectives  99.4 us (13%)
  between operations  16.1 us (2%)
  matrix products  8.66 us (1%)
    unnamed x3, waiting for transfers between devices  532 us
    psum x1, blocking collectives, late_sums(): lax.psum((jnp.sum(psi_local * psi_local), jnp.sum(psi_local * sigma_local...  99.4 us
    all_gather x1, waiting for transfers between devices, local(): gathered = lax.all_gather(wave, 'ops', axis=0, tiled=True)  91 us
  transfers between devices with their start and end apart: 2, of which 2 were waited for; matrix products, arithmetic and copies ran while one was open for 0% of the time, Pallas kernels for 0%

commit v1 on v0

v1 whole, which is shorter than its diff:
```python
import jax
import jax.numpy as jnp
from jax import lax
from jax.experimental import pallas as pl
from jax.experimental.pallas import tpu as pltpu
from jax.sharding import PartitionSpec as P

Y, Z, C, B = 4, 8, 2, 8
ROWS = 6
CAP = 384
TERMS, SECT = 2, 2
MESH = pl.DeviceIdType.MESH
BF, F32 = jnp.bfloat16, jnp.float32


def split(x):
    high = x.astype(BF)
    return high, (x - high.astype(F32)).astype(BF)


def kernel(
    ld_ref, rd_ref, wave_ref, l_hbm, r_hbm, sigma_ref, resid_ref,
    lbuf, rbuf, load_sem,
    own, g0, g1, psi, la, pb, ra, rb, sig,
    s0, s1, t0, t1, u0, u1, v0, v1, w0, w1,
    q, qb, qc, qz, qy,
    ga_s, ga_r, gb_s, gb_r, gf_s, gf_r,
    rc_s, rc_r, ra_s, ra_r, rb_s, rb_r,
    q_s, q_r,
):
    o, b = lax.axis_index("ops"), lax.axis_index("blk")
    y, z, c = o // (Z * C), lax.rem(o // C, Z), lax.rem(o, C)
    other = 1 - c

    def dev(yy, zz, cc):
        return (yy * (Z * C) + zz * C + cc, b)

    def yplus(d):
        return lax.rem(y + d, Y)

    def zplus(d):
        return lax.rem(z + d, Z)

    def remote(src, dst, send, recv, to):
        return pltpu.make_async_remote_copy(
            src_ref=src, dst_ref=dst, send_sem=send, recv_sem=recv,
            device_id=to, device_id_type=MESH,
        )

    partner = dev(y, z, other)
    to_y = [None] + [dev(yplus(d), z, c) for d in range(1, Y)]
    to_z = [None] + [dev(y, zplus(d), c) for d in range(1, Z)]
    to_b = [None] + [(o, lax.rem(b + d, B)) for d in range(1, B)]
    peers = to_y[1:] + to_z[1:] + to_b[1:] + [partner]

    barrier = pltpu.get_barrier_semaphore()
    for to in peers:
        pl.semaphore_signal(barrier, inc=1, device_id=to, device_id_type=MESH)

    loads = []
    for s in range(SECT):
        for t in range(TERMS):
            loads.append((
                pltpu.make_async_copy(l_hbm.at[t, s], lbuf.at[t, s], load_sem.at[0, t, s]),
                pltpu.make_async_copy(r_hbm.at[t, s], rbuf.at[t, s], load_sem.at[1, t, s]),
            ))
    for one, two in loads:
        one.start()
        two.start()

    row_ids = o * ROWS + lax.broadcasted_iota(jnp.int32, (ROWS, CAP), 0)
    col_ids = lax.broadcasted_iota(jnp.int32, (ROWS, CAP), 1)
    masks = []
    for s in range(SECT):
        masks.append(
            ((row_ids < ld_ref[s]) & (col_ids < rd_ref[s])).astype(F32)
        )
        for i in range(ROWS):
            own[s, i : i + 1, :] = wave_ref[i, s : s + 1, :]
        own[s] = own[s] * masks[s]
    g0[z, c, y] = own[0]
    g1[y, c, z] = own[1]
    square = own[0] * own[0] + own[1] * own[1]
    q[...] = jnp.zeros_like(q)
    q[1, 0:ROWS, :] = sum(square[:, k : k + 128] for k in range(0, CAP, 128))

    pl.semaphore_wait(barrier, len(peers))

    sends = []

    def go(copy):
        copy.start()
        sends.append(copy)

    for d in range(1, Z):
        slot = g1.at[y, c, z]
        go(remote(slot, slot, ga_s.at[d], ga_r.at[d], to_z[d]))
    for d in range(1, Y):
        slot = g0.at[z, c, y]
        go(remote(slot, slot, ga_s.at[Z + d], ga_r.at[Z + d], to_y[d]))

    def prepare_left(s):
        for t in range(TERMS):
            loads[s * TERMS + t][0].wait()
            high, low = split(lbuf[t, s])
            rows = pl.ds(t * CAP, CAP)
            la[s, rows, 0:CAP] = high
            la[s, rows, CAP : 2 * CAP] = high
            la[s, rows, 2 * CAP : 3 * CAP] = low

    def prepare_right(s):
        for t in range(TERMS):
            loads[s * TERMS + t][1].wait()
            high, low = split(jnp.transpose(rbuf[t, s]))
            at = 3 * CAP * t
            rb[s, at : at + CAP, :] = high
            rb[s, at + CAP : at + 2 * CAP, :] = low
            rb[s, at + 2 * CAP : at + 3 * CAP, :] = high

    for d in range(1, Y):
        slot = g0.at[z, c, lax.rem(y - d + Y, Y)]
        remote(slot, slot, ga_s.at[Z + d], ga_r.at[Z + d], to_y[d]).wait_recv()
    bundle = g0.at[z, c]
    for d in range(1, Z):
        go(remote(bundle, bundle, gb_s.at[d], gb_r.at[d], to_z[d]))
    go(remote(bundle, bundle, gf_s.at[0], gf_r.at[0], partner))
    for d in range(1, Z):
        slot = g1.at[y, c, lax.rem(z - d + Z, Z)]
        remote(slot, slot, ga_s.at[d], ga_r.at[d], to_z[d]).wait_recv()
    bundle = g1.at[y, c]
    for d in range(1, Y):
        go(remote(bundle, bundle, gb_s.at[Z + d], gb_r.at[Z + d], to_y[d]))
    go(remote(bundle, bundle, gf_s.at[Z], gf_r.at[Z], partner))

    for s in range(SECT):
        prepare_left(s)
        prepare_right(s)

    for d in sorted(range(1, Z), key=lambda d: min(d, Z - d)):
        slot = g0.at[lax.rem(z - d + Z, Z), c]
        remote(slot, slot, gb_s.at[d], gb_r.at[d], to_z[d]).wait_recv()
        go(remote(slot, slot, gf_s.at[d], gf_r.at[d], partner))
    for d in sorted(range(1, Y), key=lambda d: min(d, Y - d)):
        slot = g1.at[lax.rem(y - d + Y, Y), c]
        remote(slot, slot, gb_s.at[Z + d], gb_r.at[Z + d], to_y[d]).wait_recv()
        go(remote(slot, slot, gf_s.at[Z + d], gf_r.at[Z + d], partner))

    def unpack(s):
        def body(g, carry):
            yy, zp = g // (Z // 2), lax.rem(g, Z // 2)
            parts = []
            for k in range(4):
                zz, cc = 2 * zp + k // 2, k % 2
                parts.append(g0[zz, cc, yy] if s == 0 else g1[yy, cc, zz])
            at = pl.multiple_of(g * 4 * ROWS, 8)
            psi[s, pl.ds(at, 4 * ROWS), :] = jnp.concatenate(parts, axis=0)
            return carry

        lax.fori_loop(0, Y * Z // 2, body, 0)
        high, low = split(psi[s])
        pb[s, 0:CAP, :] = high
        pb[s, CAP : 2 * CAP, :] = low
        pb[s, 2 * CAP : 3 * CAP, :] = high

    def products(s):
        inner = jnp.dot(la[s], pb[s], preferred_element_type=F32)
        for t in range(TERMS):
            high, low = split(inner[t * CAP : (t + 1) * CAP])
            at = 3 * CAP * t
            ra[s, :, at : at + CAP] = high
            ra[s, :, at + CAP : at + 2 * CAP] = high
            ra[s, :, at + 2 * CAP : at + 3 * CAP] = low
        sig[s] = jnp.dot(ra[s], rb[s], preferred_element_type=F32)

    def pack(s):
        def body(g, total):
            yy, zp = g // (Z // 2), lax.rem(g, Z // 2)
            at = pl.multiple_of(g * 4 * ROWS, 8)
            block = sig[s, pl.ds(at, 4 * ROWS), :]
            pair = block * psi[s, pl.ds(at, 4 * ROWS), :]
            for i in range(0, 4 * ROWS, 8):
                for j in range(0, CAP, 128):
                    total = total + pair[i : i + 8, j : j + 128]
            for k in range(4):
                zz, cc = 2 * zp + k // 2, k % 2
                part = block[k * ROWS : (k + 1) * ROWS]
                if s == 0:
                    s0[cc, zz, yy] = part
                else:
                    s1[cc, yy, zz] = part
            return total

        return lax.fori_loop(0, Y * Z // 2, body, jnp.zeros((8, 128), F32))

    core = []
    total = None
    for s in range(SECT):
        if s == 0:
            for d in range(Z):
                slot = g0.at[lax.rem(z - d + Z, Z), other]
                remote(slot, slot, gf_s.at[d], gf_r.at[d], partner).wait_recv()
        else:
            for d in range(Y):
                slot = g1.at[lax.rem(y - d + Y, Y), other]
                remote(slot, slot, gf_s.at[Z + d], gf_r.at[Z + d], partner).wait_recv()
        unpack(s)
        products(s)
        part = pack(s)
        total = part if total is None else total + part
        src, dst = ((s0, t0), (s1, t1))[s]
        copy = remote(src.at[other], dst, rc_s.at[s], rc_r.at[s], partner)
        go(copy)
        core.append(copy)
    q[0] = total

    for d in range(1, B):
        go(remote(q, qb.at[d], q_s.at[d], q_r.at[d], to_b[d]))

    core[0].wait_recv()
    order_z = sorted(range(1, Z), key=lambda d: -min(d, Z - d))
    order_y = sorted(range(1, Y), key=lambda d: -min(d, Y - d))
    for d in order_z + [0]:
        zz = zplus(d)
        s0[c, zz] = s0[c, zz] + t0[zz]
        if d:
            go(remote(s0.at[c, zz], u0.at[d], ra_s.at[d], ra_r.at[d], to_z[d]))
    core[1].wait_recv()
    for d in order_y + [0]:
        yy = yplus(d)
        s1[c, yy] = s1[c, yy] + t1[yy]
        if d:
            go(remote(s1.at[c, yy], u1.at[d], ra_s.at[Z + d], ra_r.at[Z + d], to_y[d]))

    acc = q[...]
    for d in range(1, B):
        remote(q, qb.at[d], q_s.at[d], q_r.at[d], to_b[d]).wait_recv()
        acc = acc + qb[d]
    qb[0] = acc
    copy = remote(qb.at[0], qc.at[1], q_s.at[0], q_r.at[0], partner)
    go(copy)
    copy.wait_recv()
    acc = acc + qc[1]
    qc[0] = acc
    for d in range(1, Z):
        go(remote(qc.at[0], qz.at[d], q_s.at[B + d], q_r.at[B + d], to_z[d]))
    for d in range(1, Z):
        remote(qc.at[0], qz.at[d], q_s.at[B + d], q_r.at[B + d], to_z[d]).wait_recv()
        acc = acc + qz[d]
    qz[0] = acc
    for d in range(1, Y):
        go(remote(qz.at[0], qy.at[d], q_s.at[B + Z + d], q_r.at[B + Z + d], to_y[d]))

    tot = s0[c, z]
    for d in reversed(order_z):
        remote(s0.at[c, z], u0.at[d], ra_s.at[d], ra_r.at[d], to_z[d]).wait_recv()
        tot = tot + u0[d]
    v0[...] = tot
    for d in order_y:
        go(remote(v0.at[yplus(d)], w0.at[d], rb_s.at[Z + d], rb_r.at[Z + d], to_y[d]))
    tot = s1[c, y]
    for d in reversed(order_y):
        remote(s1.at[c, y], u1.at[d], ra_s.at[Z + d], ra_r.at[Z + d], to_y[d]).wait_recv()
        tot = tot + u1[d]
    v1[...] = tot
    for d in order_z:
        go(remote(v1.at[zplus(d)], w1.at[d], rb_s.at[d], rb_r.at[d], to_z[d]))

    for d in range(1, Y):
        remote(qz.at[0], qy.at[d], q_s.at[B + Z + d], q_r.at[B + Z + d], to_y[d]).wait_recv()
        acc = acc + qy[d]
    theta = jnp.sum(acc[0], keepdims=True) / jnp.sum(acc[1], keepdims=True)

    out0 = v0[y]
    for d in range(1, Y):
        remote(v0.at[y], w0.at[d], rb_s.at[Z + d], rb_r.at[Z + d], to_y[d]).wait_recv()
        out0 = out0 + w0[d]
    out1 = v1[z]
    for d in range(1, Z):
        remote(v1.at[z], w1.at[d], rb_s.at[d], rb_r.at[d], to_z[d]).wait_recv()
        out1 = out1 + w1[d]
    for s, out in ((0, out0), (1, out1)):
        out = out * masks[s]
        res = out - theta * own[s]
        for i in range(ROWS):
            sigma_ref[i, s : s + 1, :] = out[i : i + 1]
            resid_ref[i, s : s + 1, :] = res[i : i + 1]
    for copy in sends:
        copy.wait_send()


def local(wave, left_op, right_op, left_dims, right_dims):
    dma = pltpu.SemaphoreType.DMA
    chunk = (ROWS, CAP)
    vmem, smem = pltpu.VMEM, pltpu.SMEM
    return pl.pallas_call(
        kernel,
        out_shape=[jax.ShapeDtypeStruct((ROWS, SECT, CAP), F32)] * 2,
        in_specs=[
            pl.BlockSpec(memory_space=smem),
            pl.BlockSpec(memory_space=smem),
            pl.BlockSpec(memory_space=vmem),
            pl.BlockSpec(memory_space=pl.ANY),
            pl.BlockSpec(memory_space=pl.ANY),
        ],
        out_specs=[pl.BlockSpec(memory_space=vmem)] * 2,
        scratch_shapes=[
            vmem((TERMS, SECT, CAP, CAP), F32),
            vmem((TERMS, SECT, CAP, CAP), F32),
            dma((2, TERMS, SECT)),
            vmem((SECT,) + chunk, F32),
            vmem((Z, C, Y) + chunk, F32),
            vmem((Y, C, Z) + chunk, F32),
            vmem((SECT, CAP, CAP), F32),
            vmem((SECT, TERMS * CAP, 3 * CAP), BF),
            vmem((SECT, 3 * CAP, CAP), BF),
            vmem((SECT, CAP, 3 * TERMS * CAP), BF),
            vmem((SECT, 3 * TERMS * CAP, CAP), BF),
            vmem((SECT, CAP, CAP), F32),
            vmem((C, Z, Y) + chunk, F32),
            vmem((C, Y, Z) + chunk, F32),
            vmem((Z, Y) + chunk, F32),
            vmem((Y, Z) + chunk, F32),
            vmem((Z, Y) + chunk, F32),
            vmem((Y, Z) + chunk, F32),
            vmem((Y,) + chunk, F32),
            vmem((Z,) + chunk, F32),
            vmem((Y,) + chunk, F32),
            vmem((Z,) + chunk, F32),
            vmem((2, 8, 128), F32),
            vmem((B, 2, 8, 128), F32),
            vmem((2, 2, 8, 128), F32),
            vmem((Z, 2, 8, 128), F32),
            vmem((Y, 2, 8, 128), F32),
        ]
        + [dma((Z + Y,))] * 6
        + [dma((SECT,))] * 2
        + [dma((Z + Y,))] * 4
        + [dma((B + Z + Y,))] * 2,
        compiler_params=pltpu.CompilerParams(
            collective_id=0, has_side_effects=True, vmem_limit_bytes=48 * 1024 * 1024
        ),
        cost_estimate=pl.CostEstimate(
            flops=6_000_000_000, bytes_accessed=5_000_000, transcendentals=0
        ),
    )(left_dims, right_dims, wave, left_op, right_op)


def solution(mesh):
    in_specs = (
        P("ops", "blk", None),
        P("ops", "blk", None, None),
        P("ops", "blk", None, None),
        P("blk"),
        P("blk"),
    )
    out_specs = (P("ops", "blk", None), P("ops", "blk", None))
    return jax.shard_map(local, mesh=mesh, in_specs=in_specs, out_specs=out_specs, check_vma=False)
```

time: 756 us -> 63.8 us (0.08)
  waiting for transfers between devices: 623 us -> 0 us
  blocking collectives: 99.4 us -> 0 us
  Pallas kernels: 0 us -> 56.3 us
  between operations: 16.1 us -> 0.65 us
  matrix products: 8.66 us -> 0 us
    unnamed x3 -> x0, waiting for transfers between devices: 532 us -> none
    psum x1 -> x0, blocking collectives: 99.4 us -> none  [late_sums(): lax.psum((jnp.sum(psi_local * psi_local), jnp.sum(psi_local * sigma_local...]
    all_gather x1 -> x0, waiting for transfers between devices: 91 us -> none  [local(): gathered = lax.all_gather(wave, 'ops', axis=0, tiled=True)]
    pallas_call x0 -> x1, Pallas kernels: none -> 56.3 us  [local(): pl.pallas_call(kernel, out_shape=[jax.ShapeDtypeStruct((ROWS, SECT, CAP),...]
    dot_general x2 -> x0, matrix products: 8.66 us -> none  [the longest x1 4.7 us: local(): inner = jnp.einsum('tsik,ksj->tisj', left_op, psi_whole, precision=highest)]
  transfers between devices with their start and end apart: 2 -> 0, of which waited for: 2 -> 0; matrix products, arithmetic and copies ran while one was open for 0% -> 0% of each run, Pallas kernels for 0% -> 0%
where the time goes in v1:
time: 63.8 us; the launch traced here: 63.5 us
  Pallas kernels  56.3 us (88%)
  local copies, waits for them, and re-layouts  6.57 us (10%)
  between operations  0.65 us (1%)
    pallas_call x1, Pallas kernels, local(): pl.pallas_call(kernel, out_shape=[jax.ShapeDtypeStruct((ROWS, SECT, CAP),...  56.3 us
    unnamed x12, local copies, waits for them, and re-layouts  6.57 us

profile of v1, /device:TPU:1, one launch (start us, length us, event | category | flops | bytes accessed | tf_op | source)
XLA Modules:
  0.0 63.5 jit_solution(6000476926002204591)
XLA Ops:
  0.6 0.0 copy-start
  0.6 1.7 %copy-done = f32[2,2,384,384]{3,2,1,0:T(8,128)S(1)} copy-done((f32[2,2,384,384]{3,2,1,0:T(8,128)S(1)}, f32[2,2,384,384]{3,2,1,0:T(8,128)}, u32[]{:S(2)}) %copy-start) | copy-done | bytes 2359320
  2.3 0.0 copy-start.1
  2.3 1.7 %copy-done.1 = f32[2,2,384,384]{3,2,1,0:T(8,128)S(1)} copy-done((f32[2,2,384,384]{3,2,1,0:T(8,128)S(1)}, f32[2,2,384,384]{3,2,1,0:T(8,128)}, u32[]{:S(2)}) %copy-start.1) | copy-done | bytes 2359320
  4.0 0.0 copy-start.2
  4.0 0.7 %copy-done.2 = f32[6,2,384]{2,1,0:T(2,128)S(1)} copy-done((f32[6,2,384]{2,1,0:T(2,128)S(1)}, f32[6,2,384]{2,1,0:T(2,128)}, u32[]{:S(2)}) %copy-start.2) | copy-done | bytes 18456
  4.7 0.0 copy-start.3
  4.7 0.7 %copy-done.3 = s32[2]{0:T(128)S(1)} copy-done((s32[2]{0:T(128)S(1)}, s32[2]{0:T(128)}, u32[]{:S(2)}) %copy-start.3) | copy-done | bytes 32
  5.3 0.0 copy-start.4
  5.3 0.7 %copy-done.4 = s32[2]{0:T(128)S(1)} copy-done((s32[2]{0:T(128)S(1)}, s32[2]{0:T(128)}, u32[]{:S(2)}) %copy-start.4) | copy-done | bytes 32
  6.0 56.3 %shard_map.68 = (f32[6,2,384]{2,1,0:T(2,128)S(1)}, f32[6,2,384]{2,1,0:T(2,128)S(1)}) custom-call(s32[2]{0:T(128)S(1)} %copy-done.3, s32[2]{0:T(128)S(1)} %copy-done.4, f32[6,2,384]{2,1,0:T(2,128)S(1)} %copy-done.2, f32[2,2,384,384]{3,2,1,0:T(8,128)S(1)} %copy-done, f32[2,2,384,384]{3,2,1,0:T(8,128)S(1)} %copy-done.1), custom_call_target="tpu_custom_call" | custom-call | flops 6000000000 | bytes 5000000 | tf_op jit(solution)/shard_map/pallas_call | solution.py:295
  62.3 0.6 copy.9
  62.9 0.6 copy.10
Async XLA Ops:
  0.6 1.7 %copy-start = (f32[2,2,384,384]{3,2,1,0:T(8,128)S(1)}, f32[2,2,384,384]{3,2,1,0:T(8,128)}, u32[]{:S(2)}) copy-start(f32[2,2,384,384]{3,2,1,0:T(8,128)} %l_hbm.1) | copy-start | bytes 7077892
  2.3 1.7 %copy-start.1 = (f32[2,2,384,384]{3,2,1,0:T(8,128)S(1)}, f32[2,2,384,384]{3,2,1,0:T(8,128)}, u32[]{:S(2)}) copy-start(f32[2,2,384,384]{3,2,1,0:T(8,128)} %r_hbm.1) | copy-start | bytes 7077892
  4.0 0.7 %copy-start.2 = (f32[6,2,384]{2,1,0:T(2,128)S(1)}, f32[6,2,384]{2,1,0:T(2,128)}, u32[]{:S(2)}) copy-start(f32[6,2,384]{2,1,0:T(2,128)} %wave_ref.1) | copy-start | bytes 55300
  4.7 0.7 %copy-start.3 = (s32[2]{0:T(128)S(1)}, s32[2]{0:T(128)}, u32[]{:S(2)}) copy-start(s32[2]{0:T(128)} %ld_ref.1) | copy-start | bytes 28
  5.3 0.7 %copy-start.4 = (s32[2]{0:T(128)S(1)}, s32[2]{0:T(128)}, u32[]{:S(2)}) copy-start(s32[2]{0:T(128)} %rd_ref.1) | copy-start | bytes 28

commit v2 on v0

v2 whole, which is shorter than its diff:
```python
import jax
import jax.numpy as jnp
from jax import lax
from jax.experimental import pallas as pl
from jax.experimental.pallas import tpu as pltpu
from jax.sharding import PartitionSpec as P

Y, Z, C, B = 4, 8, 2, 8
ROWS = 6
CAP = 384
TERMS, SECT = 2, 2
MESH = pl.DeviceIdType.MESH
BF, F32 = jnp.bfloat16, jnp.float32


def split(x):
    high = x.astype(BF)
    return high, (x - high.astype(F32)).astype(BF)


def kernel(
    ld_hbm, rd_hbm, wave_hbm, l_hbm, r_hbm, sigma_ref, resid_ref,
    ld_ref, rd_ref, wave_ref, in_sem,
    lbuf, rbuf, load_sem,
    own, near, ga, gb, psi, la, pb, ra, rb, sig,
    sa, sb, ta, tb, ua, ub, vl, wl, fin,
    q, qb, qh, ql,
    li_s, li_r, hi_s, hi_r, fa_s, fa_r, fb_s, fb_r,
    co_s, co_r, ho_s, ho_r, lo_s, lo_r,
    qb_s, qb_r, qh_s, qh_r, ql_s, ql_r,
):
    small = [
        pltpu.make_async_copy(wave_hbm, wave_ref, in_sem.at[0]),
        pltpu.make_async_copy(ld_hbm, ld_ref, in_sem.at[1]),
        pltpu.make_async_copy(rd_hbm, rd_ref, in_sem.at[2]),
    ]
    for copy in small:
        copy.start()

    o, b = lax.axis_index("ops"), lax.axis_index("blk")
    y, z, c = o // (Z * C), lax.rem(o // C, Z), lax.rem(o, C)
    other = 1 - c
    yp = [lax.rem(y + d, Y) for d in range(Y)]
    ym = [lax.rem(y - d + Y, Y) for d in range(Y)]
    zp = [lax.rem(z + d, Z) for d in range(Z)]
    zm = [lax.rem(z - d + Z, Z) for d in range(Z)]

    def dev(yy, zz, cc, bb):
        return (yy * (Z * C) + zz * C + cc, bb)

    def remote(src, dst, send, recv, to):
        return pltpu.make_async_remote_copy(
            src_ref=src, dst_ref=dst, send_sem=send, recv_sem=recv,
            device_id=to, device_id_type=MESH,
        )

    partner = dev(y, z, other, b)
    to_y = [dev(yp[d], z, c, b) for d in range(Y)]
    to_z = [dev(y, zp[d], c, b) for d in range(Z)]
    to_b = [
        dev(y, z, other if k % 2 else c, lax.rem(b + k // 2, B)) for k in range(2 * B)
    ]
    peers = to_y[1:] + to_z[1:] + to_b[1:]

    barrier = pltpu.get_barrier_semaphore()
    for to in peers:
        pl.semaphore_signal(barrier, inc=1, device_id=to, device_id_type=MESH)

    loads = [
        [
            (
                pltpu.make_async_copy(l_hbm.at[t, s], lbuf.at[t, s], load_sem.at[0, t, s]),
                pltpu.make_async_copy(r_hbm.at[t, s], rbuf.at[t, s], load_sem.at[1, t, s]),
            )
            for t in range(TERMS)
        ]
        for s in range(SECT)
    ]
    for s in range(SECT):
        for t in range(TERMS):
            loads[s][t][0].start()
            loads[s][t][1].start()

    row_ids = o * ROWS + lax.broadcasted_iota(jnp.int32, (ROWS, CAP), 0)
    col_ids = lax.broadcasted_iota(jnp.int32, (ROWS, CAP), 1)
    for copy in small:
        copy.wait()
    masks = []
    me = y * other + z * c
    for s in range(SECT):
        masks.append(
            ((row_ids < ld_ref[s]) & (col_ids < rd_ref[s])).astype(F32)
        )
        for i in range(ROWS):
            own[s, i : i + 1, :] = wave_ref[i, s : s + 1, :]
        own[s] = own[s] * masks[s]
        near[me, s] = own[s]

    pl.semaphore_wait(barrier, len(peers))

    class Path:
        pass

    one, two = Path(), Path()
    one.light, one.heavy, one.light_m, one.heavy_m = to_y, to_z, ym, zm
    one.light_p, one.heavy_p = yp, zp
    one.light_me, one.heavy_me = y, z
    one.g, one.s, one.t, one.u, one.f_s, one.f_r = ga, sa, ta, ua, fa_s, fa_r
    two.light, two.heavy, two.light_m, two.heavy_m = to_z, to_y, zm, ym
    two.light_p, two.heavy_p = zp, yp
    two.light_me, two.heavy_me = z, y
    two.g, two.s, two.t, two.u, two.f_s, two.f_r = gb, sb, tb, ub, fb_s, fb_r
    for p, o_ in ((one, two), (two, one)):
        p.other = o_
        p.n, p.m = len(p.light), len(p.heavy)
        p.near_first = sorted(range(1, p.m), key=lambda d: min(d, p.m - d))
        p.far_first = p.near_first[::-1]
    sends = []

    def both(step, *args):
        @pl.when(c == 0)
        def _():
            step(one, *args)

        @pl.when(c == 1)
        def _():
            step(two, *args)

    def go(copy):
        copy.start()

    def gather_start(p):
        slot = near.at[p.light_me]
        for d in range(1, p.n):
            go(remote(slot, slot, li_s.at[d], li_r.at[d], p.light[d]))
        for d in range(1, p.n):
            slot = near.at[p.light_m[d]]
            remote(slot, slot, li_s.at[d], li_r.at[d], p.light[d]).wait_recv()
        for s in range(SECT):
            for k in range(p.n):
                p.g[s, p.heavy_me, k * ROWS : (k + 1) * ROWS, :] = near[k, s]
            slot = p.g.at[s, p.heavy_me]
            for d in p.far_first:
                go(remote(slot, slot, hi_s.at[s, d], hi_r.at[s, d], p.heavy[d]))
            go(remote(slot, slot, p.f_s.at[s, 0], p.f_r.at[s, 0], partner))

    def gather_forward(p, s):
        for d in p.near_first:
            slot = p.g.at[s, p.heavy_m[d]]
            remote(slot, slot, hi_s.at[s, d], hi_r.at[s, d], p.heavy[d]).wait_recv()
            go(remote(slot, slot, p.f_s.at[s, d], p.f_r.at[s, d], partner))

    def gather_finish(p, s):
        p = p.other
        for d in range(p.m):
            slot = p.g.at[s, p.heavy_m[d]]
            remote(slot, slot, p.f_s.at[s, d], p.f_r.at[s, d], partner).wait_recv()

    def prepare(s):
        for t in range(TERMS):
            loads[s][t][0].wait()
            high, low = split(lbuf[t, s])
            rows = pl.ds(t * CAP, CAP)
            la[s, rows, 0:CAP] = high
            la[s, rows, CAP : 2 * CAP] = high
            la[s, rows, 2 * CAP : 3 * CAP] = low
        for t in range(TERMS):
            loads[s][t][1].wait()
            high, low = split(jnp.transpose(rbuf[t, s]))
            at = 3 * CAP * t
            rb[s, at : at + CAP, :] = high
            rb[s, at + CAP : at + 2 * CAP, :] = low
            rb[s, at + 2 * CAP : at + 3 * CAP, :] = high

    def unpack(s):
        for g in range(Y * Z // 4):
            yy = g // 2
            parts = []
            for zz in range(4 * (g % 2), 4 * (g % 2) + 4):
                parts.append(ga[s, zz, yy * ROWS : (yy + 1) * ROWS, :])
                parts.append(gb[s, yy, zz * ROWS : (zz + 1) * ROWS, :])
            block = jnp.concatenate(parts, axis=0)
            at, n = g * 8 * ROWS, 8 * ROWS
            psi[s, at : at + n, :] = block
            high, low = split(block)
            pb[s, at : at + n, :] = high
            pb[s, CAP + at : CAP + at + n, :] = low
            pb[s, 2 * CAP + at : 2 * CAP + at + n, :] = high

    def first_product(s):
        inner = jnp.dot(la[s], pb[s], preferred_element_type=F32)
        for t in range(TERMS):
            high, low = split(inner[t * CAP : (t + 1) * CAP])
            at = 3 * CAP * t
            ra[s, :, at : at + CAP] = high
            ra[s, :, at + CAP : at + 2 * CAP] = high
            ra[s, :, at + 2 * CAP : at + 3 * CAP] = low

    def second_product(s):
        sig[s] = jnp.dot(ra[s], rb[s], preferred_element_type=F32)

    def pack(s):
        for g in range(Y * Z // 2):
            yy = g // 4
            at, n = g * 4 * ROWS, 4 * ROWS
            block = sig[s, at : at + n, :]
            for k in range(4):
                zz, cc = 2 * (g % 4) + k // 2, k % 2
                part = block[k * ROWS : (k + 1) * ROWS]
                if cc == 0:
                    sa[s, zz, yy * ROWS : (yy + 1) * ROWS, :] = part
                else:
                    sb[s, yy, zz * ROWS : (zz + 1) * ROWS, :] = part

    def core_start(p, s):
        r = p.other
        go(remote(r.s.at[s], r.t.at[s], co_s.at[s], co_r.at[s], partner))

    def correlate(s):
        def body(i, total):
            rows = pl.ds(pl.multiple_of(i * 16, 16), 16)
            pair = sig[s, rows, :] * psi[s, rows, :]
            for i in (0, 8):
                for j in range(0, CAP, 128):
                    total = total + pair[i : i + 8, j : j + 128]
            return total

        return lax.fori_loop(0, CAP // 16, body, jnp.zeros((8, 128), F32))

    def scatter_start(p, s):
        remote(p.s.at[s], p.t.at[s], co_s.at[s], co_r.at[s], partner).wait_recv()
        for d in p.far_first + [0]:
            at = p.heavy_p[d]
            p.s[s, at] = p.s[s, at] + p.t[s, at]
            if d:
                go(remote(p.s.at[s, at], p.u.at[s, d], ho_s.at[s, d], ho_r.at[s, d], p.heavy[d]))

    def scalars_start(p):
        for d in p.far_first:
            go(remote(qh.at[0], qh.at[d], qh_s.at[d], qh_r.at[d], p.heavy[d]))

    def scatter_sum(p, s):
        total = p.s[s, p.heavy_me]
        for d in p.near_first:
            remote(p.s.at[s, 0], p.u.at[s, d], ho_s.at[s, d], ho_r.at[s, d], p.heavy[d]).wait_recv()
            total = total + p.u[s, d]
        for k in range(p.n):
            vl[k, s] = total[k * ROWS : (k + 1) * ROWS]

    def scatter_finish(p):
        order = sorted(range(1, p.n), key=lambda d: -min(d, p.n - d))
        for d in order:
            go(remote(vl.at[p.light_p[d]], wl.at[d], lo_s.at[d], lo_r.at[d], p.light[d]))
        total = qh[0]
        for d in range(1, p.m):
            remote(qh.at[0], qh.at[d], qh_s.at[d], qh_r.at[d], p.heavy[d]).wait_recv()
            total = total + qh[d]
        ql[0] = total
        for d in order:
            go(remote(ql.at[0], ql.at[d], ql_s.at[d], ql_r.at[d], p.light[d]))
        out = vl[p.light_me]
        for d in order[::-1]:
            remote(vl.at[0], wl.at[d], lo_s.at[d], lo_r.at[d], p.light[d]).wait_recv()
            out = out + wl[d]
        fin[...] = out
        for d in order[::-1]:
            remote(ql.at[0], ql.at[d], ql_s.at[d], ql_r.at[d], p.light[d]).wait_recv()
            total = total + ql[d]
        q[...] = total

    both(gather_start)
    square = own[0] * own[0] + own[1] * own[1]
    q[...] = jnp.zeros_like(q)
    q[1, 0:ROWS, :] = sum(square[:, k : k + 128] for k in range(0, CAP, 128))
    for s in range(SECT):
        prepare(s)
    both(gather_forward, 0)
    both(gather_finish, 0)
    unpack(0)
    first_product(0)
    both(gather_forward, 1)
    second_product(0)
    pack(0)
    both(core_start, 0)
    both(gather_finish, 1)
    unpack(1)
    first_product(1)
    both(scatter_start, 0)
    second_product(1)
    pack(1)
    both(core_start, 1)
    q[0] = correlate(0) + correlate(1)
    for k in range(1, 2 * B):
        copy = remote(q, qb.at[k], qb_s.at[k], qb_r.at[k], to_b[k])
        copy.start()
        sends.append(copy)
    both(scatter_start, 1)
    total = q[...]
    for k in range(1, 2 * B):
        remote(q, qb.at[k], qb_s.at[k], qb_r.at[k], to_b[k]).wait_recv()
        total = total + qb[k]
    qh[0] = total
    for copy in sends:
        copy.wait_send()
    both(scalars_start)
    both(scatter_sum, 0)
    both(scatter_sum, 1)
    both(scatter_finish)

    theta = jnp.sum(q[0], keepdims=True) / jnp.sum(q[1], keepdims=True)
    for s in range(SECT):
        out = fin[s] * masks[s]
        res = out - theta * own[s]
        for i in range(ROWS):
            sigma_ref[i, s : s + 1, :] = out[i : i + 1]
            resid_ref[i, s : s + 1, :] = res[i : i + 1]

    def finish(p):
        for d in range(1, p.n):
            remote(near.at[0], near.at[0], li_s.at[d], li_r.at[d], partner).wait_send()
            remote(vl.at[0], wl.at[d], lo_s.at[d], lo_r.at[d], partner).wait_send()
            remote(ql.at[0], ql.at[d], ql_s.at[d], ql_r.at[d], partner).wait_send()
        for d in range(1, p.m):
            remote(qh.at[0], qh.at[d], qh_s.at[d], qh_r.at[d], partner).wait_send()
        for s in range(SECT):
            slot, r = p.g.at[s, 0], p.other
            for d in range(p.m):
                remote(slot, slot, p.f_s.at[s, d], p.f_r.at[s, d], partner).wait_send()
            for d in range(1, p.m):
                remote(slot, slot, hi_s.at[s, d], hi_r.at[s, d], partner).wait_send()
                remote(p.s.at[s, 0], p.u.at[s, d], ho_s.at[s, d], ho_r.at[s, d], partner).wait_send()
            remote(r.s.at[s], r.t.at[s], co_s.at[s], co_r.at[s], partner).wait_send()

    both(finish)


def local(wave, left_op, right_op, left_dims, right_dims):
    dma = pltpu.SemaphoreType.DMA
    chunk = (ROWS, CAP)
    vmem, smem = pltpu.VMEM, pltpu.SMEM
    return pl.pallas_call(
        kernel,
        out_shape=[jax.ShapeDtypeStruct((ROWS, SECT, CAP), F32)] * 2,
        in_specs=[pl.BlockSpec(memory_space=pltpu.HBM)] * 5,
        out_specs=[pl.BlockSpec(memory_space=vmem)] * 2,
        scratch_shapes=[
            smem((SECT,), jnp.int32),
            smem((SECT,), jnp.int32),
            vmem((ROWS, SECT, CAP), F32),
            dma((3,)),
            vmem((TERMS, SECT, CAP, CAP), F32),
            vmem((TERMS, SECT, CAP, CAP), F32),
            dma((2, TERMS, SECT)),
            vmem((SECT,) + chunk, F32),
            vmem((Z, SECT) + chunk, F32),
            vmem((SECT, Z, Y * ROWS, CAP), F32),
            vmem((SECT, Y, Z * ROWS, CAP), F32),
            vmem((SECT, CAP, CAP), F32),
            vmem((SECT, TERMS * CAP, 3 * CAP), BF),
            vmem((SECT, 3 * CAP, CAP), BF),
            vmem((SECT, CAP, 3 * TERMS * CAP), BF),
            vmem((SECT, 3 * TERMS * CAP, CAP), BF),
            vmem((SECT, CAP, CAP), F32),
        ]
        + [vmem((SECT, Z, Y * ROWS, CAP), F32), vmem((SECT, Y, Z * ROWS, CAP), F32)] * 3
        + [
            vmem((Z, SECT) + chunk, F32),
            vmem((Z, SECT) + chunk, F32),
            vmem((SECT,) + chunk, F32),
            vmem((2, 8, 128), F32),
            vmem((2 * B, 2, 8, 128), F32),
            vmem((Z, 2, 8, 128), F32),
            vmem((Z, 2, 8, 128), F32),
        ]
        + [dma((Z,))] * 2
        + [dma((SECT, Z))] * 6
        + [dma((SECT,))] * 2
        + [dma((SECT, Z))] * 2
        + [dma((Z,))] * 2
        + [dma((2 * B,))] * 2
        + [dma((Z,))] * 4,
        compiler_params=pltpu.CompilerParams(
            collective_id=0, has_side_effects=True, vmem_limit_bytes=64 * 1024 * 1024
        ),
        cost_estimate=pl.CostEstimate(
            flops=6_000_000_000, bytes_accessed=5_000_000, transcendentals=0
        ),
    )(left_dims, right_dims, wave, left_op, right_op)


def solution(mesh):
    in_specs = (
        P("ops", "blk", None),
        P("ops", "blk", None, None),
        P("ops", "blk", None, None),
        P("blk"),
        P("blk"),
    )
    out_specs = (P("ops", "blk", None), P("ops", "blk", None))
    return jax.shard_map(local, mesh=mesh, in_specs=in_specs, out_specs=out_specs, check_vma=False)
```

time: 756 us -> 55.8 us (0.07)
  waiting for transfers between devices: 623 us -> 0 us
  blocking collectives: 99.4 us -> 0 us
  Pallas kernels: 0 us -> 51.4 us
  between operations: 16.1 us -> 0.64 us
  matrix products: 8.66 us -> 0 us
    unnamed x3 -> x0, waiting for transfers between devices: 532 us -> none
    psum x1 -> x0, blocking collectives: 99.4 us -> none  [late_sums(): lax.psum((jnp.sum(psi_local * psi_local), jnp.sum(psi_local * sigma_local...]
    all_gather x1 -> x0, waiting for transfers between devices: 91 us -> none  [local(): gathered = lax.all_gather(wave, 'ops', axis=0, tiled=True)]
    pallas_call x0 -> x1, Pallas kernels: none -> 51.4 us  [local(): pl.pallas_call(kernel, out_shape=[jax.ShapeDtypeStruct((ROWS, SECT, CAP),...]
    dot_general x2 -> x0, matrix products: 8.66 us -> none  [the longest x1 4.7 us: local(): inner = jnp.einsum('tsik,ksj->tisj', left_op, psi_whole, precision=highest)]
  transfers between devices with their start and end apart: 2 -> 0, of which waited for: 2 -> 0; matrix products, arithmetic and copies ran while one was open for 0% -> 0% of each run, Pallas kernels for 0% -> 0%
where the time goes in v2:
time: 55.8 us; the launch traced here: 54.7 us
  Pallas kernels  51.4 us (92%)
  local copies, waits for them, and re-layouts  2.66 us (5%)
  between operations  0.64 us (1%)
    pallas_call x1, Pallas kernels, local(): pl.pallas_call(kernel, out_shape=[jax.ShapeDtypeStruct((ROWS, SECT, CAP),...  51.4 us
    unnamed x2, local copies, waits for them, and re-layouts  2.66 us

profile of v2, /device:TPU:1, one launch (start us, length us, event | category | flops | bytes accessed | tf_op | source)
XLA Modules:
  0.0 54.7 jit_solution(3305984538902473884)
XLA Ops:
  0.6 51.4 %shard_map.68 = (f32[6,2,384]{2,1,0:T(2,128)}, f32[6,2,384]{2,1,0:T(2,128)}) custom-call(s32[2]{0:T(128)} %ld_hbm.1, s32[2]{0:T(128)} %rd_hbm.1, f32[6,2,384]{2,1,0:T(2,128)} %wave_hbm.1, f32[2,2,384,384]{3,2,1,0:T(8,128)} %l_hbm.1, f32[2,2,384,384]{3,2,1,0:T(8,128)} %r_hbm.1), custom_call_target="tpu_custom_call" | custom-call | flops 6000000000 | bytes 5000000 | tf_op jit(solution)/shard_map/pallas_call | solution.py:341
  52.1 1.3 %copy.9 = f32[6,2,384]{2,1,0:T(2,128)} copy(f32[6,2,384]{2,1,0:T(2,128)} %get-tuple-element.4) | data formatting | bytes 36864
  53.4 1.3 %copy.10 = f32[6,2,384]{2,1,0:T(2,128)} copy(f32[6,2,384]{2,1,0:T(2,128)} %get-tuple-element.5) | data formatting | bytes 36864

commit v3 on v2

--- a/solution.py
+++ b/solution.py
@@ -19,7 +19,7 @@
 
 
 def kernel(
-    ld_hbm, rd_hbm, wave_hbm, l_hbm, r_hbm, sigma_ref, resid_ref,
+    ld_hbm, rd_hbm, wave_hbm, l_hbm, r_hbm, raw_ref, mask_ref, shift_ref,
     ld_ref, rd_ref, wave_ref, in_sem,
     lbuf, rbuf, load_sem,
     own, near, ga, gb, psi, la, pb, ra, rb, sig,
@@ -76,11 +76,6 @@
         ]
         for s in range(SECT)
     ]
-    for s in range(SECT):
-        for t in range(TERMS):
-            loads[s][t][0].start()
-            loads[s][t][1].start()
-
     row_ids = o * ROWS + lax.broadcasted_iota(jnp.int32, (ROWS, CAP), 0)
     col_ids = lax.broadcasted_iota(jnp.int32, (ROWS, CAP), 1)
     for copy in small:
@@ -88,9 +83,7 @@
     masks = []
     me = y * other + z * c
     for s in range(SECT):
-        masks.append(
-            ((row_ids < ld_ref[s]) & (col_ids < rd_ref[s])).astype(F32)
-        )
+        masks.append(((row_ids < ld_ref[s]) & (col_ids < rd_ref[s])).astype(F32))
         for i in range(ROWS):
             own[s, i : i + 1, :] = wave_ref[i, s : s + 1, :]
         own[s] = own[s] * masks[s]
@@ -115,7 +108,6 @@
         p.n, p.m = len(p.light), len(p.heavy)
         p.near_first = sorted(range(1, p.m), key=lambda d: min(d, p.m - d))
         p.far_first = p.near_first[::-1]
-    sends = []
 
     def both(step, *args):
         @pl.when(c == 0)
@@ -133,6 +125,8 @@
         slot = near.at[p.light_me]
         for d in range(1, p.n):
             go(remote(slot, slot, li_s.at[d], li_r.at[d], p.light[d]))
+
+    def gather_heavy(p):
         for d in range(1, p.n):
             slot = near.at[p.light_m[d]]
             remote(slot, slot, li_s.at[d], li_r.at[d], p.light[d]).wait_recv()
@@ -227,6 +221,23 @@
 
         return lax.fori_loop(0, CAP // 16, body, jnp.zeros((8, 128), F32))
 
+    def gather_sent(p):
+        for d in range(1, p.n):
+            remote(near.at[0], near.at[0], li_s.at[d], li_r.at[d], partner).wait_send()
+        for s in range(SECT):
+            slot = p.g.at[s, 0]
+            for d in range(p.m):
+                remote(slot, slot, p.f_s.at[s, d], p.f_r.at[s, d], partner).wait_send()
+            for d in range(1, p.m):
+                remote(slot, slot, hi_s.at[s, d], hi_r.at[s, d], partner).wait_send()
+
+    def scatter_sent(p):
+        r = p.other
+        for s in range(SECT):
+            for d in range(1, p.m):
+                remote(p.s.at[s, 0], p.u.at[s, d], ho_s.at[s, d], ho_r.at[s, d], partner).wait_send()
+            remote(r.s.at[s], r.t.at[s], co_s.at[s], co_r.at[s], partner).wait_send()
+
     def scatter_start(p, s):
         remote(p.s.at[s], p.t.at[s], co_s.at[s], co_r.at[s], partner).wait_recv()
         for d in p.far_first + [0]:
@@ -237,7 +248,7 @@
 
     def scalars_start(p):
         for d in p.far_first:
-            go(remote(qh.at[0], qh.at[d], qh_s.at[d], qh_r.at[d], p.heavy[d]))
+            go(remote(qh.at[0], qh.at[d], qh_s.at[0], qh_r.at[0], p.heavy[d]))
 
     def scatter_sum(p, s):
         total = p.s[s, p.heavy_me]
@@ -252,26 +263,37 @@
         for d in order:
             go(remote(vl.at[p.light_p[d]], wl.at[d], lo_s.at[d], lo_r.at[d], p.light[d]))
         total = qh[0]
+        rest = qh.at[pl.ds(1, p.m - 1)]
+        remote(rest, rest, qh_s.at[0], qh_r.at[0], partner).wait()
         for d in range(1, p.m):
-            remote(qh.at[0], qh.at[d], qh_s.at[d], qh_r.at[d], p.heavy[d]).wait_recv()
             total = total + qh[d]
         ql[0] = total
         for d in order:
-            go(remote(ql.at[0], ql.at[d], ql_s.at[d], ql_r.at[d], p.light[d]))
+            go(remote(ql.at[0], ql.at[d], ql_s.at[0], ql_r.at[0], p.light[d]))
+        scatter_sent(p)
         out = vl[p.light_me]
         for d in order[::-1]:
-            remote(vl.at[0], wl.at[d], lo_s.at[d], lo_r.at[d], p.light[d]).wait_recv()
+            remote(vl.at[0], wl.at[d], lo_s.at[d], lo_r.at[d], p.light[d]).wait()
             out = out + wl[d]
         fin[...] = out
-        for d in order[::-1]:
-            remote(ql.at[0], ql.at[d], ql_s.at[d], ql_r.at[d], p.light[d]).wait_recv()
+        rest = ql.at[pl.ds(1, p.n - 1)]
+        remote(rest, rest, ql_s.at[0], ql_r.at[0], partner).wait()
+        for d in range(1, p.n):
             total = total + ql[d]
         q[...] = total
 
     both(gather_start)
+    for s in range(SECT):
+        for t in range(TERMS):
+            loads[s][t][0].start()
+            loads[s][t][1].start()
     square = own[0] * own[0] + own[1] * own[1]
-    q[...] = jnp.zeros_like(q)
-    q[1, 0:ROWS, :] = sum(square[:, k : k + 128] for k in range(0, CAP, 128))
+    square = sum(square[:, k : k + 128] for k in range(0, CAP, 128))
+    q[1:2, :] = jnp.sum(square, axis=0, keepdims=True)
+    for s in range(SECT):
+        for i in range(ROWS):
+            mask_ref[i, s : s + 1, :] = masks[s][i : i + 1]
+    both(gather_heavy)
     for s in range(SECT):
         prepare(s)
     both(gather_forward, 0)
@@ -286,66 +308,44 @@
     unpack(1)
     first_product(1)
     both(scatter_start, 0)
+    first = correlate(0)
     second_product(1)
+    q[0:1, :] = jnp.sum(first + correlate(1), axis=0, keepdims=True)
+    for k in range(1, 2 * B):
+        go(remote(q, qb.at[k], qb_s.at[0], qb_r.at[0], to_b[k]))
     pack(1)
     both(core_start, 1)
-    q[0] = correlate(0) + correlate(1)
-    for k in range(1, 2 * B):
-        copy = remote(q, qb.at[k], qb_s.at[k], qb_r.at[k], to_b[k])
-        copy.start()
-        sends.append(copy)
     both(scatter_start, 1)
+    both(gather_sent)
+    rest = qb.at[pl.ds(1, 2 * B - 1)]
+    remote(rest, rest, qb_s.at[0], qb_r.at[0], partner).wait()
     total = q[...]
     for k in range(1, 2 * B):
-        remote(q, qb.at[k], qb_s.at[k], qb_r.at[k], to_b[k]).wait_recv()
         total = total + qb[k]
     qh[0] = total
-    for copy in sends:
-        copy.wait_send()
     both(scalars_start)
     both(scatter_sum, 0)
     both(scatter_sum, 1)
     both(scatter_finish)
 
-    theta = jnp.sum(q[0], keepdims=True) / jnp.sum(q[1], keepdims=True)
+    theta = jnp.sum(q[0:1, :], axis=1, keepdims=True) / jnp.sum(q[1:2, :], axis=1, keepdims=True)
     for s in range(SECT):
-        out = fin[s] * masks[s]
-        res = out - theta * own[s]
         for i in range(ROWS):
-            sigma_ref[i, s : s + 1, :] = out[i : i + 1]
-            resid_ref[i, s : s + 1, :] = res[i : i + 1]
-
-    def finish(p):
-        for d in range(1, p.n):
-            remote(near.at[0], near.at[0], li_s.at[d], li_r.at[d], partner).wait_send()
-            remote(vl.at[0], wl.at[d], lo_s.at[d], lo_r.at[d], partner).wait_send()
-            remote(ql.at[0], ql.at[d], ql_s.at[d], ql_r.at[d], partner).wait_send()
-        for d in range(1, p.m):
-            remote(qh.at[0], qh.at[d], qh_s.at[d], qh_r.at[d], partner).wait_send()
-        for s in range(SECT):
-            slot, r = p.g.at[s, 0], p.other
-            for d in range(p.m):
-                remote(slot, slot, p.f_s.at[s, d], p.f_r.at[s, d], partner).wait_send()
-            for d in range(1, p.m):
-                remote(slot, slot, hi_s.at[s, d], hi_r.at[s, d], partner).wait_send()
-                remote(p.s.at[s, 0], p.u.at[s, d], ho_s.at[s, d], ho_r.at[s, d], partner).wait_send()
-            remote(r.s.at[s], r.t.at[s], co_s.at[s], co_r.at[s], partner).wait_send()
-
-    both(finish)
-
+            raw_ref[i, s : s + 1, :] = fin[s, i : i + 1]
+            shift_ref[i, s : s + 1, :] = theta * own[s, i : i + 1]
 
 def local(wave, left_op, right_op, left_dims, right_dims):
     dma = pltpu.SemaphoreType.DMA
     chunk = (ROWS, CAP)
-    vmem, smem = pltpu.VMEM, pltpu.SMEM
-    return pl.pallas_call(
+    vmem = pltpu.VMEM
+    raw, mask, shift = pl.pallas_call(
         kernel,
-        out_shape=[jax.ShapeDtypeStruct((ROWS, SECT, CAP), F32)] * 2,
+        out_shape=[jax.ShapeDtypeStruct((ROWS, SECT, CAP), F32)] * 3,
         in_specs=[pl.BlockSpec(memory_space=pltpu.HBM)] * 5,
-        out_specs=[pl.BlockSpec(memory_space=vmem)] * 2,
+        out_specs=[pl.BlockSpec(memory_space=vmem)] * 3,
         scratch_shapes=[
-            smem((SECT,), jnp.int32),
-            smem((SECT,), jnp.int32),
+            pltpu.SMEM((SECT,), jnp.int32),
+            pltpu.SMEM((SECT,), jnp.int32),
             vmem((ROWS, SECT, CAP), F32),
             dma((3,)),
             vmem((TERMS, SECT, CAP, CAP), F32),
@@ -367,18 +367,17 @@
             vmem((Z, SECT) + chunk, F32),
             vmem((Z, SECT) + chunk, F32),
             vmem((SECT,) + chunk, F32),
-            vmem((2, 8, 128), F32),
-            vmem((2 * B, 2, 8, 128), F32),
-            vmem((Z, 2, 8, 128), F32),
-            vmem((Z, 2, 8, 128), F32),
+            vmem((2, 128), F32),
+            vmem((2 * B, 2, 128), F32),
+            vmem((Z, 2, 128), F32),
+            vmem((Z, 2, 128), F32),
         ]
         + [dma((Z,))] * 2
         + [dma((SECT, Z))] * 6
         + [dma((SECT,))] * 2
         + [dma((SECT, Z))] * 2
         + [dma((Z,))] * 2
-        + [dma((2 * B,))] * 2
-        + [dma((Z,))] * 4,
+        + [dma((1,))] * 6,
         compiler_params=pltpu.CompilerParams(
             collective_id=0, has_side_effects=True, vmem_limit_bytes=64 * 1024 * 1024
         ),
@@ -386,6 +385,8 @@
             flops=6_000_000_000, bytes_accessed=5_000_000, transcendentals=0
         ),
     )(left_dims, right_dims, wave, left_op, right_op)
+    sigma = raw * mask
+    return sigma, sigma - shift
 
 
 def solution(mesh):

time: 55.8 us -> 51.4 us (0.921)
  local copies, waits for them, and re-layouts: 2.66 us -> 0 us
  Pallas kernels: 51.4 us -> 48.8 us
  other arithmetic: 0 us -> 1.38 us
    pallas_call x1, Pallas kernels: 51.4 us -> 48.8 us  [local(): pl.pallas_call(kernel, out_shape=[jax.ShapeDtypeStruct((ROWS, SECT, CAP),...]
    unnamed x2 -> x0, local copies, waits for them, and re-layouts: 2.66 us -> none
    sub x0 -> x1, other arithmetic: none -> 1.38 us  [local(): return (sigma, sigma - shift)]
where the time goes in v3:
time: 51.4 us; the launch traced here: 50.8 us
  Pallas kernels  48.8 us (95%)
  other arithmetic  1.38 us (3%)
  between operations  0.64 us (1%)
    pallas_call x1, Pallas kernels, local(): pl.pallas_call(kernel, out_shape=[jax.ShapeDtypeStruct((ROWS, SECT, CAP),...  48.8 us
    sub x1, other arithmetic, local(): return (sigma, sigma - shift)  1.38 us

profile of v3, /device:TPU:1, one launch (start us, length us, event | category | flops | bytes accessed | tf_op | source)
XLA Modules:
  0.0 50.8 jit_solution(13753722862094730614)
XLA Ops:
  0.6 48.8 %shard_map.68 = (f32[6,2,384]{2,1,0:T(2,128)}, f32[6,2,384]{2,1,0:T(2,128)}, f32[6,2,384]{2,1,0:T(2,128)}) custom-call(s32[2]{0:T(128)} %ld_hbm.1, s32[2]{0:T(128)} %rd_hbm.1, f32[6,2,384]{2,1,0:T(2,128)} %wave_hbm.1, f32[2,2,384,384]{3,2,1,0:T(8,128)} %l_hbm.1, f32[2,2,384,384]{3,2,1,0:T(8,128)} %r_hbm.1), custom_call_target="tpu_custom_call" | custom-call | flops 6000000000 | bytes 5000000 | tf_op jit(solution)/shard_map/pallas_call | solution.py:341
  49.4 1.4 %fusion = (f32[6,2,384]{2,1,0:T(2,128)}, f32[6,2,384]{2,1,0:T(2,128)}) fusion(f32[6,2,384]{2,1,0:T(2,128)} %get-tuple-element.7, f32[6,2,384]{2,1,0:T(2,128)} %get-tuple-element.5, f32[6,2,384]{2,1,0:T(2,128)} %get-tuple-element.6), kind=kLoop, calls=%fused_computation | loop fusion | flops 9216 | bytes 92160 | tf_op jit(solution)/shard_map/sub | solution.py:389

commit v4 on v3

--- a/solution.py
+++ b/solution.py
@@ -20,7 +20,7 @@
 
 def kernel(
     ld_hbm, rd_hbm, wave_hbm, l_hbm, r_hbm, raw_ref, mask_ref, shift_ref,
-    ld_ref, rd_ref, wave_ref, in_sem,
+    ld_ref, rd_ref, in_sem,
     lbuf, rbuf, load_sem,
     own, near, ga, gb, psi, la, pb, ra, rb, sig,
     sa, sb, ta, tb, ua, ub, vl, wl, fin,
@@ -29,17 +29,19 @@
     co_s, co_r, ho_s, ho_r, lo_s, lo_r,
     qb_s, qb_r, qh_s, qh_r, ql_s, ql_r,
 ):
+    o, b = lax.axis_index("ops"), lax.axis_index("blk")
+    y, z, c = o // (Z * C), lax.rem(o // C, Z), lax.rem(o, C)
+    other = 1 - c
+    me = y * other + z * c
+
     small = [
-        pltpu.make_async_copy(wave_hbm, wave_ref, in_sem.at[0]),
+        pltpu.make_async_copy(wave_hbm, near.at[me], in_sem.at[0]),
         pltpu.make_async_copy(ld_hbm, ld_ref, in_sem.at[1]),
         pltpu.make_async_copy(rd_hbm, rd_ref, in_sem.at[2]),
     ]
     for copy in small:
         copy.start()
 
-    o, b = lax.axis_index("ops"), lax.axis_index("blk")
-    y, z, c = o // (Z * C), lax.rem(o // C, Z), lax.rem(o, C)
-    other = 1 - c
     yp = [lax.rem(y + d, Y) for d in range(Y)]
     ym = [lax.rem(y - d + Y, Y) for d in range(Y)]
     zp = [lax.rem(z + d, Z) for d in range(Z)]
@@ -76,25 +78,14 @@
         ]
         for s in range(SECT)
     ]
-    row_ids = o * ROWS + lax.broadcasted_iota(jnp.int32, (ROWS, CAP), 0)
-    col_ids = lax.broadcasted_iota(jnp.int32, (ROWS, CAP), 1)
-    for copy in small:
-        copy.wait()
-    masks = []
-    me = y * other + z * c
-    for s in range(SECT):
-        masks.append(((row_ids < ld_ref[s]) & (col_ids < rd_ref[s])).astype(F32))
-        for i in range(ROWS):
-            own[s, i : i + 1, :] = wave_ref[i, s : s + 1, :]
-        own[s] = own[s] * masks[s]
-        near[me, s] = own[s]
-
     pl.semaphore_wait(barrier, len(peers))
 
     class Path:
         pass
 
     one, two = Path(), Path()
+    one.row, one.gap = (z * C + c) * ROWS, (Z * C - 1) * ROWS
+    two.row, two.gap = (y * Z * C + c) * ROWS, (C - 1) * ROWS
     one.light, one.heavy, one.light_m, one.heavy_m = to_y, to_z, ym, zm
     one.light_p, one.heavy_p = yp, zp
     one.light_me, one.heavy_me = y, z
@@ -122,21 +113,29 @@
         copy.start()
 
     def gather_start(p):
-        slot = near.at[p.light_me]
         for d in range(1, p.n):
-            go(remote(slot, slot, li_s.at[d], li_r.at[d], p.light[d]))
+            go(remote(wave_hbm, near.at[p.light_me], li_s.at[d], li_r.at[d], p.light[d]))
 
     def gather_heavy(p):
         for d in range(1, p.n):
             slot = near.at[p.light_m[d]]
             remote(slot, slot, li_s.at[d], li_r.at[d], p.light[d]).wait_recv()
+        size = (p.n * ROWS, CAP)
+        at, row = lax.broadcasted_iota(jnp.int32, size, 0), p.row
+        row = row + at + sum((at >= k * ROWS).astype(jnp.int32) for k in range(1, p.n)) * p.gap
+        col = lax.broadcasted_iota(jnp.int32, size, 1)
         for s in range(SECT):
             for k in range(p.n):
-                p.g[s, p.heavy_me, k * ROWS : (k + 1) * ROWS, :] = near[k, s]
-            slot = p.g.at[s, p.heavy_me]
-            for d in p.far_first:
-                go(remote(slot, slot, hi_s.at[s, d], hi_r.at[s, d], p.heavy[d]))
-            go(remote(slot, slot, p.f_s.at[s, 0], p.f_r.at[s, 0], partner))
+                for i in range(ROWS):
+                    p.g[s, p.heavy_me, k * ROWS + i : k * ROWS + i + 1, :] = near[k, i, s : s + 1, :]
+            inside = (row < ld_ref[s]) & (col < rd_ref[s])
+            p.g[s, p.heavy_me] = jnp.where(inside, p.g[s, p.heavy_me], 0.0)
+
+    def gather_bundle(p, s):
+        slot = p.g.at[s, p.heavy_me]
+        for d in p.far_first:
+            go(remote(slot, slot, hi_s.at[s, d], hi_r.at[s, d], p.heavy[d]))
+        go(remote(slot, slot, p.f_s.at[s, 0], p.f_r.at[s, 0], partner))
 
     def gather_forward(p, s):
         for d in p.near_first:
@@ -223,7 +222,7 @@
 
     def gather_sent(p):
         for d in range(1, p.n):
-            remote(near.at[0], near.at[0], li_s.at[d], li_r.at[d], partner).wait_send()
+            remote(wave_hbm, near.at[0], li_s.at[d], li_r.at[d], partner).wait_send()
         for s in range(SECT):
             slot = p.g.at[s, 0]
             for d in range(p.m):
@@ -287,6 +286,16 @@
         for t in range(TERMS):
             loads[s][t][0].start()
             loads[s][t][1].start()
+    row_ids = o * ROWS + lax.broadcasted_iota(jnp.int32, (ROWS, CAP), 0)
+    col_ids = lax.broadcasted_iota(jnp.int32, (ROWS, CAP), 1)
+    for copy in small:
+        copy.wait()
+    masks = []
+    for s in range(SECT):
+        masks.append(((row_ids < ld_ref[s]) & (col_ids < rd_ref[s])).astype(F32))
+        for i in range(ROWS):
+            own[s, i : i + 1, :] = near[me, i, s : s + 1, :]
+        own[s] = own[s] * masks[s]
     square = own[0] * own[0] + own[1] * own[1]
     square = sum(square[:, k : k + 128] for k in range(0, CAP, 128))
     q[1:2, :] = jnp.sum(square, axis=0, keepdims=True)
@@ -294,8 +303,10 @@
         for i in range(ROWS):
             mask_ref[i, s : s + 1, :] = masks[s][i : i + 1]
     both(gather_heavy)
-    for s in range(SECT):
-        prepare(s)
+    both(gather_bundle, 0)
+    prepare(0)
+    both(gather_bundle, 1)
+    prepare(1)
     both(gather_forward, 0)
     both(gather_finish, 0)
     unpack(0)
@@ -346,13 +357,12 @@
         scratch_shapes=[
             pltpu.SMEM((SECT,), jnp.int32),
             pltpu.SMEM((SECT,), jnp.int32),
-            vmem((ROWS, SECT, CAP), F32),
             dma((3,)),
             vmem((TERMS, SECT, CAP, CAP), F32),
             vmem((TERMS, SECT, CAP, CAP), F32),
             dma((2, TERMS, SECT)),
             vmem((SECT,) + chunk, F32),
-            vmem((Z, SECT) + chunk, F32),
+            vmem((Z, ROWS, SECT, CAP), F32),
             vmem((SECT, Z, Y * ROWS, CAP), F32),
             vmem((SECT, Y, Z * ROWS, CAP), F32),
             vmem((SECT, CAP, CAP), F32),

time: 51.4 us -> 50.5 us (0.982)
  Pallas kernels: 48.8 us -> 48.1 us
    pallas_call x1, Pallas kernels: 48.8 us -> 48.1 us  [local(): pl.pallas_call(kernel, out_shape=[jax.ShapeDtypeStruct((ROWS, SECT, CAP),...]
where the time goes in v4:
time: 50.5 us; the launch traced here: 50.1 us
  Pallas kernels  48.1 us (95%)
  other arithmetic  1.38 us (3%)
  between operations  0.64 us (1%)
    pallas_call x1, Pallas kernels, local(): pl.pallas_call(kernel, out_shape=[jax.ShapeDtypeStruct((ROWS, SECT, CAP),...  48.1 us
    sub x1, other arithmetic, local(): return (sigma, sigma - shift)  1.38 us

profile of v4, /device:TPU:1, one launch (start us, length us, event | category | flops | bytes accessed | tf_op | source)
XLA Modules:
  0.0 50.1 jit_solution(1338985509384343560)
XLA Ops:
  0.6 48.1 %shard_map.68 = (f32[6,2,384]{2,1,0:T(2,128)}, f32[6,2,384]{2,1,0:T(2,128)}, f32[6,2,384]{2,1,0:T(2,128)}) custom-call(s32[2]{0:T(128)} %ld_hbm.1, s32[2]{0:T(128)} %rd_hbm.1, f32[6,2,384]{2,1,0:T(2,128)} %wave_hbm.1, f32[2,2,384,384]{3,2,1,0:T(8,128)} %l_hbm.1, f32[2,2,384,384]{3,2,1,0:T(8,128)} %r_hbm.1), custom_call_target="tpu_custom_call" | custom-call | flops 6000000000 | bytes 5000000 | tf_op jit(solution)/shard_map/pallas_call | solution.py:352
  48.7 1.4 %fusion = (f32[6,2,384]{2,1,0:T(2,128)}, f32[6,2,384]{2,1,0:T(2,128)}) fusion(f32[6,2,384]{2,1,0:T(2,128)} %get-tuple-element.7, f32[6,2,384]{2,1,0:T(2,128)} %get-tuple-element.5, f32[6,2,384]{2,1,0:T(2,128)} %get-tuple-element.6), kind=kLoop, calls=%fused_computation | loop fusion | flops 9216 | bytes 92160 | tf_op jit(solution)/shard_map/sub | solution.py:399

commit v5 on v4

--- a/solution.py
+++ b/solution.py
@@ -23,7 +23,7 @@
     ld_ref, rd_ref, in_sem,
     lbuf, rbuf, load_sem,
     own, near, ga, gb, psi, la, pb, ra, rb, sig,
-    sa, sb, ta, tb, ua, ub, vl, wl, fin,
+    sa, sb, ta, tb, ua, ub, vl, wl,
     q, qb, qh, ql,
     li_s, li_r, hi_s, hi_r, fa_s, fa_r, fb_s, fb_r,
     co_s, co_r, ho_s, ho_r, lo_s, lo_r,
@@ -62,7 +62,8 @@
     to_b = [
         dev(y, z, other if k % 2 else c, lax.rem(b + k // 2, B)) for k in range(2 * B)
     ]
-    peers = to_y[1:] + to_z[1:] + to_b[1:]
+    peers = [to_z[4], to_y[2], to_z[3], to_z[5]] + to_b[8:12] + to_b[4:8] + to_b[12:]
+    peers += [to_y[1], to_y[3], to_z[2], to_z[6]] + to_b[2:4] + [to_z[1], to_z[7], to_b[1]]
 
     barrier = pltpu.get_barrier_semaphore()
     for to in peers:
@@ -114,12 +115,11 @@
 
     def gather_start(p):
         for d in range(1, p.n):
-            go(remote(wave_hbm, near.at[p.light_me], li_s.at[d], li_r.at[d], p.light[d]))
+            go(remote(wave_hbm, near.at[p.light_me], li_s.at[0], li_r.at[0], p.light[d]))
 
     def gather_heavy(p):
-        for d in range(1, p.n):
-            slot = near.at[p.light_m[d]]
-            remote(slot, slot, li_s.at[d], li_r.at[d], p.light[d]).wait_recv()
+        rest = near.at[pl.ds(1, p.n - 1)]
+        remote(rest, rest, li_s.at[0], li_r.at[0], partner).wait_recv()
         size = (p.n * ROWS, CAP)
         at, row = lax.broadcasted_iota(jnp.int32, size, 0), p.row
         row = row + at + sum((at >= k * ROWS).astype(jnp.int32) for k in range(1, p.n)) * p.gap
@@ -134,20 +134,19 @@
     def gather_bundle(p, s):
         slot = p.g.at[s, p.heavy_me]
         for d in p.far_first:
-            go(remote(slot, slot, hi_s.at[s, d], hi_r.at[s, d], p.heavy[d]))
-        go(remote(slot, slot, p.f_s.at[s, 0], p.f_r.at[s, 0], partner))
+            go(remote(slot, slot, hi_s.at[s], hi_r.at[s], p.heavy[d]))
+
+    def rest_of(buf, s, n):
+        return buf.at[s, pl.ds(1, n - 1)]
 
     def gather_forward(p, s):
-        for d in p.near_first:
-            slot = p.g.at[s, p.heavy_m[d]]
-            remote(slot, slot, hi_s.at[s, d], hi_r.at[s, d], p.heavy[d]).wait_recv()
-            go(remote(slot, slot, p.f_s.at[s, d], p.f_r.at[s, d], partner))
+        rest = rest_of(p.g, s, p.m)
+        remote(rest, rest, hi_s.at[s], hi_r.at[s], partner).wait_recv()
+        go(remote(p.g.at[s], p.g.at[s], p.f_s.at[s], p.f_r.at[s], partner))
 
     def gather_finish(p, s):
         p = p.other
-        for d in range(p.m):
-            slot = p.g.at[s, p.heavy_m[d]]
-            remote(slot, slot, p.f_s.at[s, d], p.f_r.at[s, d], partner).wait_recv()
+        remote(p.g.at[s], p.g.at[s], p.f_s.at[s], p.f_r.at[s], partner).wait_recv()
 
     def prepare(s):
         for t in range(TERMS):
@@ -221,20 +220,18 @@
         return lax.fori_loop(0, CAP // 16, body, jnp.zeros((8, 128), F32))
 
     def gather_sent(p):
-        for d in range(1, p.n):
-            remote(wave_hbm, near.at[0], li_s.at[d], li_r.at[d], partner).wait_send()
+        rest = near.at[pl.ds(1, p.n - 1)]
+        remote(rest, rest, li_s.at[0], li_r.at[0], partner).wait_send()
         for s in range(SECT):
-            slot = p.g.at[s, 0]
-            for d in range(p.m):
-                remote(slot, slot, p.f_s.at[s, d], p.f_r.at[s, d], partner).wait_send()
-            for d in range(1, p.m):
-                remote(slot, slot, hi_s.at[s, d], hi_r.at[s, d], partner).wait_send()
+            rest = rest_of(p.g, s, p.m)
+            remote(rest, rest, hi_s.at[s], hi_r.at[s], partner).wait_send()
+            remote(p.g.at[s], p.g.at[s], p.f_s.at[s], p.f_r.at[s], partner).wait_send()
 
     def scatter_sent(p):
         r = p.other
         for s in range(SECT):
-            for d in range(1, p.m):
-                remote(p.s.at[s, 0], p.u.at[s, d], ho_s.at[s, d], ho_r.at[s, d], partner).wait_send()
+            rest = rest_of(p.u, s, p.m)
+            remote(rest, rest, ho_s.at[s], ho_r.at[s], partner).wait_send()
             remote(r.s.at[s], r.t.at[s], co_s.at[s], co_r.at[s], partner).wait_send()
 
     def scatter_start(p, s):
@@ -243,7 +240,7 @@
             at = p.heavy_p[d]
             p.s[s, at] = p.s[s, at] + p.t[s, at]
             if d:
-                go(remote(p.s.at[s, at], p.u.at[s, d], ho_s.at[s, d], ho_r.at[s, d], p.heavy[d]))
+                go(remote(p.s.at[s, at], p.u.at[s, d], ho_s.at[s], ho_r.at[s], p.heavy[d]))
 
     def scalars_start(p):
         for d in p.far_first:
@@ -251,8 +248,9 @@
 
     def scatter_sum(p, s):
         total = p.s[s, p.heavy_me]
-        for d in p.near_first:
-            remote(p.s.at[s, 0], p.u.at[s, d], ho_s.at[s, d], ho_r.at[s, d], p.heavy[d]).wait_recv()
+        rest = rest_of(p.u, s, p.m)
+        remote(rest, rest, ho_s.at[s], ho_r.at[s], partner).wait_recv()
+        for d in range(1, p.m):
             total = total + p.u[s, d]
         for k in range(p.n):
             vl[k, s] = total[k * ROWS : (k + 1) * ROWS]
@@ -260,7 +258,7 @@
     def scatter_finish(p):
         order = sorted(range(1, p.n), key=lambda d: -min(d, p.n - d))
         for d in order:
-            go(remote(vl.at[p.light_p[d]], wl.at[d], lo_s.at[d], lo_r.at[d], p.light[d]))
+            go(remote(vl.at[p.light_p[d]], wl.at[d], lo_s.at[0], lo_r.at[0], p.light[d]))
         total = qh[0]
         rest = qh.at[pl.ds(1, p.m - 1)]
         remote(rest, rest, qh_s.at[0], qh_r.at[0], partner).wait()
@@ -269,12 +267,16 @@
         ql[0] = total
         for d in order:
             go(remote(ql.at[0], ql.at[d], ql_s.at[0], ql_r.at[0], p.light[d]))
+        gather_sent(p)
         scatter_sent(p)
         out = vl[p.light_me]
-        for d in order[::-1]:
-            remote(vl.at[0], wl.at[d], lo_s.at[d], lo_r.at[d], p.light[d]).wait()
+        rest = wl.at[pl.ds(1, p.n - 1)]
+        remote(rest, rest, lo_s.at[0], lo_r.at[0], partner).wait()
+        for d in range(1, p.n):
             out = out + wl[d]
-        fin[...] = out
+        for s in range(SECT):
+            for i in range(ROWS):
+                raw_ref[i, s : s + 1, :] = out[s, i : i + 1]
         rest = ql.at[pl.ds(1, p.n - 1)]
         remote(rest, rest, ql_s.at[0], ql_r.at[0], partner).wait()
         for d in range(1, p.n):
@@ -327,7 +329,6 @@
     pack(1)
     both(core_start, 1)
     both(scatter_start, 1)
-    both(gather_sent)
     rest = qb.at[pl.ds(1, 2 * B - 1)]
     remote(rest, rest, qb_s.at[0], qb_r.at[0], partner).wait()
     total = q[...]
@@ -342,7 +343,6 @@
     theta = jnp.sum(q[0:1, :], axis=1, keepdims=True) / jnp.sum(q[1:2, :], axis=1, keepdims=True)
     for s in range(SECT):
         for i in range(ROWS):
-            raw_ref[i, s : s + 1, :] = fin[s, i : i + 1]
             shift_ref[i, s : s + 1, :] = theta * own[s, i : i + 1]
 
 def local(wave, left_op, right_op, left_dims, right_dims):
@@ -376,16 +376,13 @@
         + [
             vmem((Z, SECT) + chunk, F32),
             vmem((Z, SECT) + chunk, F32),
-            vmem((SECT,) + chunk, F32),
             vmem((2, 128), F32),
             vmem((2 * B, 2, 128), F32),
             vmem((Z, 2, 128), F32),
             vmem((Z, 2, 128), F32),
         ]
         + [dma((Z,))] * 2
-        + [dma((SECT, Z))] * 6
-        + [dma((SECT,))] * 2
-        + [dma((SECT, Z))] * 2
+        + [dma((SECT,))] * 10
         + [dma((Z,))] * 2
         + [dma((1,))] * 6,
         compiler_params=pltpu.CompilerParams(

time: 50.5 us -> 49.8 us (0.986)
  Pallas kernels: 48.1 us -> 47.2 us
    pallas_call x1, Pallas kernels: 48.1 us -> 47.2 us  [local(): pl.pallas_call(kernel, out_shape=[jax.ShapeDtypeStruct((ROWS, SECT, CAP),...]
where the time goes in v5:
time: 49.8 us; the launch traced here: 49.2 us
  Pallas kernels  47.2 us (95%)
  other arithmetic  1.38 us (3%)
  between operations  0.64 us (1%)
    pallas_call x1, Pallas kernels, local(): pl.pallas_call(kernel, out_shape=[jax.ShapeDtypeStruct((ROWS, SECT, CAP),...  47.2 us
    sub x1, other arithmetic, local(): return (sigma, sigma - shift)  1.38 us

profile of v5, /device:TPU:1, one launch (start us, length us, event | category | flops | bytes accessed | tf_op | source)
XLA Modules:
  0.0 49.2 jit_solution(25717008139841345)
XLA Ops:
  0.6 47.2 %shard_map.68 = (f32[6,2,384]{2,1,0:T(2,128)}, f32[6,2,384]{2,1,0:T(2,128)}, f32[6,2,384]{2,1,0:T(2,128)}) custom-call(s32[2]{0:T(128)} %ld_hbm.1, s32[2]{0:T(128)} %rd_hbm.1, f32[6,2,384]{2,1,0:T(2,128)} %wave_hbm.1, f32[2,2,384,384]{3,2,1,0:T(8,128)} %l_hbm.1, f32[2,2,384,384]{3,2,1,0:T(8,128)} %r_hbm.1), custom_call_target="tpu_custom_call" | custom-call | flops 6000000000 | bytes 5000000 | tf_op jit(solution)/shard_map/pallas_call | solution.py:352
  47.8 1.4 %fusion = (f32[6,2,384]{2,1,0:T(2,128)}, f32[6,2,384]{2,1,0:T(2,128)}) fusion(f32[6,2,384]{2,1,0:T(2,128)} %get-tuple-element.7, f32[6,2,384]{2,1,0:T(2,128)} %get-tuple-element.5, f32[6,2,384]{2,1,0:T(2,128)} %get-tuple-element.6), kind=kLoop, calls=%fused_computation | loop fusion | flops 9216 | bytes 92160 | tf_op jit(solution)/shard_map/sub | solution.py:396
